TPU v7x, 256 devices: a whole 4x4x8 slice. The times are simulated.
256 devices in a mesh: attn: 16 (over y_lo, x, core), ffn: 8 (over z), grp: 2 (over y_hi).
Axes of the slice: x: 4, y: 4 (y_hi: 2, y_lo: 2; y = y_hi * 2 + y_lo), z: 8, core: 2. Of those that a mesh axis runs over, the one named last changes fastest.
Arguments:
- query: bfloat16 [2048, 8192], P(('grp', 'attn'), 'ffn'), parts along dimension 0, may hold values from -5 to 5
- key_store_cache: bfloat16 [2048, 192, 1024], P(('grp', 'attn'), None, 'ffn'), parts along dimension 0, may hold values from -5 to 5
- value_store_cache: bfloat16 [2048, 192, 1024], P(('grp', 'attn'), None, 'ffn'), parts along dimension 0, may hold values from -5 to 5
- token_keys: bfloat16 [2048, 1024], P(('grp', 'attn'), 'ffn'), parts along dimension 0, may hold values from -5 to 5
- token_values: bfloat16 [2048, 1024], P(('grp', 'attn'), 'ffn'), parts along dimension 0, may hold values from -5 to 5
- pooled_block_keys: bfloat16 [512, 16, 1024], P(('grp', 'attn'), None, 'ffn'), parts along dimension 0, may hold values from -5 to 5
- pooled_block_values: bfloat16 [512, 16, 1024], P(('grp', 'attn'), None, 'ffn'), parts along dimension 0, may hold values from -6 to 6
- block_dst: int32 [512, 1], P('grp'), parts along dimension 0, may hold values from 0 to 15; in each aligned block of 16 rows (0 to 15, 16 to 31, ...) at most 2 rows name the same one
- block_row: int32 [512], P('grp'), parts along dimension 0, may hold values from 0 to 63
- ctx_len: int32 [2048], P(('grp', 'attn')), parts along dimension 0, may hold values from 1 to 192, as said below
- residual: bfloat16 [2048, 8192], P('grp', 'attn'), parts along dimension 0, may hold values from -15 to 15
- norm_gain: float32 [8192], P('attn'), may hold values from 0.1 to 1.9
- output_weight: bfloat16 [8192, 8192], P('ffn', 'attn'), may hold values from -0.1875 to 0.1875
- w_gate: bfloat16 [8192, 14336], P('attn', 'ffn'), may hold values from -0.0625 to 0.0625
- w_up: bfloat16 [8192, 14336], P('attn', 'ffn'), may hold values from -0.0625 to 0.0625
- w_down: bfloat16 [14336, 8192], P('ffn', 'attn'), may hold values from -0.046875 to 0.046875
Outputs:
- layer_out: bfloat16 [2048, 8192], P(('grp', 'ffn'), 'attn'), parts along dimension 0
There are 2 independent parts, one for each index of `grp`. A program takes and returns all parts, laid end to end along the dimension named above; an argument that names none is the same for every part. Nothing has to cross between parts.
Inputs may be any that keep to these rules, and one draw needn't show every extreme that they name: `block_dst`: of the 16 blocks held by one pool index (aligned blocks of rows), at most 2 name the same attention index. `ctx_len`: every attention index holds a request that uses all 192 cached positions.
All inputs are finite; a program needn't handle non-finite values.
Results may differ from a plain program's by a relative error of at most 0.024.
Values may be sent and summed in bfloat16 or wider, within the bound.
No kernel may reach another device: no remote copies, remote signals or barrier semaphores. Data moves between devices by JAX's collectives and lax.ppermute only.
A program may use at most 128 MiB of HBM per device.

v0:
```python
import jax
import jax.numpy as jnp
from jax import lax
from jax.sharding import PartitionSpec as P

MODEL_WIDTH = 8192
QUERY_HEADS = 64
KEY_VALUE_HEADS = 8
HEAD_SIZE = 128
CAP = 2
epsilon = 1e-05


def body(
    query,
    key_store_cache,
    value_store_cache,
    token_keys,
    token_values,
    pooled_block_keys,
    pooled_block_values,
    block_dst,
    block_row,
    ctx_len,
    residual,
    norm_gain,
    output_weight,
    w_gate,
    w_up,
    w_down,
):
    tok_rows = query.shape[0]
    ctx_size = key_store_cache.shape[1]
    head_width = key_store_cache.shape[2]
    groups = head_width // HEAD_SIZE
    group_rows = QUERY_HEADS // KEY_VALUE_HEADS
    block_len = pooled_block_keys.shape[1]
    local_pool = pooled_block_keys.shape[0]
    attn_size = lax.axis_size("attn")
    my_index = lax.axis_index("attn")
    slot_count = attn_size * CAP
    dst_table = block_dst[:, 0].reshape(attn_size, local_pool)
    row_table = block_row.reshape(attn_size, local_pool)
    positions = jnp.arange(local_pool, dtype=jnp.int32)
    earlier = positions[None, :] < positions[:, None]
    same_dst = dst_table[:, :, None] == dst_table[:, None, :]
    rank_table = jnp.sum((same_dst & earlier[None]).astype(jnp.int32), axis=2)
    own_dst = lax.dynamic_index_in_dim(dst_table, my_index, 0, keepdims=False)
    own_rank = lax.dynamic_index_in_dim(rank_table, my_index, 0, keepdims=False)
    slot_index = own_dst * CAP + own_rank
    picker = (jnp.arange(slot_count, dtype=jnp.int32)[:, None] == slot_index[None, :]).astype(
        jnp.bfloat16
    )
    flat_keys = pooled_block_keys.reshape(local_pool, block_len * head_width)
    flat_values = pooled_block_values.reshape(local_pool, block_len * head_width)
    send_keys = (
        jnp.dot(picker, flat_keys, preferred_element_type=jnp.float32)
        .astype(jnp.bfloat16)
        .reshape(slot_count, block_len, head_width)
    )
    send_values = (
        jnp.dot(picker, flat_values, preferred_element_type=jnp.float32)
        .astype(jnp.bfloat16)
        .reshape(slot_count, block_len, head_width)
    )
    recv_keys, recv_values = (
        lax.all_to_all(send_keys, "attn", split_axis=0, concat_axis=0, tiled=True),
        lax.all_to_all(send_values, "attn", split_axis=0, concat_axis=0, tiled=True),
    )
    cap_slots = jnp.arange(CAP, dtype=jnp.int32)
    hit_mask = (dst_table == my_index)[:, None, :] & (
        rank_table[:, None, :] == cap_slots[None, :, None]
    )
    recv_row = (jnp.sum(jnp.where(hit_mask, row_table[:, None, :] + 1, 0), axis=2) - 1).reshape(
        slot_count
    )
    score_scale = HEAD_SIZE ** (-0.5)
    query_rows = query.reshape(tok_rows, groups, group_rows, HEAD_SIZE)
    stored_keys = key_store_cache.reshape(tok_rows, ctx_size, groups, HEAD_SIZE)
    stored_values = value_store_cache.reshape(tok_rows, ctx_size, groups, HEAD_SIZE)
    score_cache = (
        jnp.einsum("bghd,btgd->bght", query_rows, stored_keys, preferred_element_type=jnp.float32)
        * score_scale
    )
    valid_mask = jnp.arange(ctx_size, dtype=jnp.int32)[None, :] < ctx_len[:, None]
    score_cache = jnp.where(valid_mask[:, None, None, :], score_cache, -jnp.inf)
    resumed_keys = recv_keys.reshape(slot_count * block_len, groups, HEAD_SIZE)
    resumed_values = recv_values.reshape(slot_count * block_len, groups, HEAD_SIZE)
    score_recv = (
        jnp.einsum("bghd,tgd->bght", query_rows, resumed_keys, preferred_element_type=jnp.float32)
        * score_scale
    )
    owner_mask = (
        jnp.repeat(recv_row, block_len)[None, :] == jnp.arange(tok_rows, dtype=jnp.int32)[:, None]
    )
    score_recv = jnp.where(owner_mask[:, None, None, :], score_recv, -jnp.inf)
    current_keys = token_keys.reshape(tok_rows, groups, HEAD_SIZE)
    score_new = (
        jnp.einsum("bghd,bgd->bgh", query_rows, current_keys, preferred_element_type=jnp.float32)
        * score_scale
    )
    row_max = jnp.maximum(
        jnp.maximum(jnp.max(score_cache, axis=-1), jnp.max(score_recv, axis=-1)), score_new
    )
    exp_cache = jnp.exp(score_cache - row_max[..., None])
    exp_recv = jnp.exp(score_recv - row_max[..., None])
    exp_new = jnp.exp(score_new - row_max)
    denominator = jnp.sum(exp_cache, axis=-1) + jnp.sum(exp_recv, axis=-1) + exp_new
    prob_cache = (exp_cache / denominator[..., None]).astype(jnp.bfloat16)
    prob_recv = (exp_recv / denominator[..., None]).astype(jnp.bfloat16)
    prob_new = (exp_new / denominator).astype(jnp.bfloat16)
    weighted = jnp.einsum(
        "bght,btgd->bghd", prob_cache, stored_values, preferred_element_type=jnp.float32
    )
    weighted = weighted + jnp.einsum(
        "bght,tgd->bghd", prob_recv, resumed_values, preferred_element_type=jnp.float32
    )
    current_values = token_values.reshape(tok_rows, groups, HEAD_SIZE).astype(jnp.float32)
    weighted = weighted + prob_new.astype(jnp.float32)[..., None] * current_values[:, :, None, :]
    attended = weighted.reshape(tok_rows, groups * group_rows * HEAD_SIZE).astype(jnp.bfloat16)
    head_part = jnp.dot(
        lax.all_gather(attended, "attn", axis=0, tiled=True),
        output_weight,
        preferred_element_type=jnp.float32,
    )
    ffn_size = lax.axis_size("ffn")
    ffn_index = lax.axis_index("ffn")
    share_rows = head_part.shape[0] // ffn_size
    attn_out = lax.psum(head_part.astype(jnp.bfloat16), "ffn").astype(jnp.float32)
    mixed = residual.astype(jnp.float32) + attn_out
    squares = lax.psum(jnp.sum(mixed * mixed, axis=1), "attn")
    normed = (mixed * lax.rsqrt(squares / MODEL_WIDTH + epsilon)[:, None] * norm_gain).astype(
        jnp.bfloat16
    )
    kept_rows = lax.dynamic_slice_in_dim(mixed, ffn_index * share_rows, share_rows, 0)
    hidden_width = w_gate.shape[1]
    gate_up = lax.psum_scatter(
        jnp.concatenate(
            [
                jnp.dot(normed, w_gate, preferred_element_type=jnp.float32),
                jnp.dot(normed, w_up, preferred_element_type=jnp.float32),
            ],
            axis=1,
        ).astype(jnp.bfloat16),
        "attn",
        scatter_dimension=0,
        tiled=True,
    ).astype(jnp.float32)
    activated = (jax.nn.silu(gate_up[:, :hidden_width]) * gate_up[:, hidden_width:]).astype(
        jnp.bfloat16
    )
    down_part = jnp.dot(
        lax.all_gather(activated, "attn", axis=0, tiled=True),
        w_down,
        preferred_element_type=jnp.float32,
    )
    ffn_share = lax.psum_scatter(
        down_part.astype(jnp.bfloat16), "ffn", scatter_dimension=0, tiled=True
    ).astype(jnp.float32)
    return (kept_rows + ffn_share).astype(jnp.bfloat16)


def solution(mesh):
    placed = (
        P(("grp", "attn"), "ffn"),
        P(("grp", "attn"), None, "ffn"),
        P(("grp", "attn"), None, "ffn"),
        P(("grp", "attn"), "ffn"),
        P(("grp", "attn"), "ffn"),
        P(("grp", "attn"), None, "ffn"),
        P(("grp", "attn"), None, "ffn"),
        P("grp", None),
        P("grp"),
        P(("grp", "attn")),
        P("grp", "attn"),
        P("attn"),
        P("ffn", "attn"),
        P("attn", "ffn"),
        P("attn", "ffn"),
        P("ffn", "attn"),
    )
    return jax.shard_map(
        body, mesh=mesh, in_specs=placed, out_specs=P(("grp", "ffn"), "attn"), check_vma=False
    )
```

profile of v0, /device:TPU:2, one launch (start us, length us, event | category | flops | bytes accessed | tf_op | source)
XLA Modules:
  0.0 378.0 jit_solution(17119664770401599803)
XLA Ops:
  6.5 0.5 broadcast.96
  7.1 1.6 reduce.9
  8.7 0.4 convert_reduce_fusion
  9.2 1.0 fusion.6
  10.2 0.7 copy.58
  10.9 5.9 %all-to-all-start = ((bf16[32,16,128]{2,1,0:T(8,128)(2,1)}), bf16[32,16,128]{2,1,0:T(8,128)(2,1)S(1)}, u32[]{:S(2)}, u32[]{:S(2)}) async-start(bf16[32,16,128]{2,1,0:T(8,128)(2,1)} %bitcast.24), calls=%async_computation | async-start | bytes 262144 | tf_op jit(solution)/shard_map/all_to_all | solution.py:67
  16.8 0.7 broadcast_add_fusion.1
  17.5 0.1 select_reduce_fusion
  17.6 0.1 copy.43
  17.7 0.1 sub.28
  17.9 0.7 eq.78
  18.6 0.7 iota_compare_fusion.1
  19.3 1.3 convert_element_type.71
  20.6 1.0 fusion.7
  21.6 0.7 copy.60
  22.3 0.9 copy.56
  23.2 0.9 fusion.21
  24.2 0.7 copy.52
  24.8 3.2 fusion.30
  28.0 0.8 copy.45
  28.8 0.7 iota_compare_fusion
  29.5 5.7 %all-to-all-start.1 = ((bf16[32,16,128]{2,1,0:T(8,128)(2,1)}), bf16[32,16,128]{2,1,0:T(8,128)(2,1)}, u32[]{:S(2)}, u32[]{:S(2)}) async-start(bf16[32,16,128]{2,1,0:T(8,128)(2,1)} %bitcast.28), calls=%async_computation.1 | async-start | bytes 262144 | tf_op jit(solution)/shard_map/all_to_all | solution.py:68
  35.3 1.3 fusion.31
  36.6 0.7 maximum_maximum_fusion
  37.3 0.1 copy.46
  37.4 1.5 fusion.8
  38.9 1.3 fusion.11
  40.3 0.1 copy.48
  40.4 3.1 convolution_bitcast_fusion.1
  43.5 1.1 fusion.10
  44.6 0.1 copy.50
  44.7 1.5 fusion.5
  46.2 0.7 copy.81
  47.0 38.8 %all-gather.3.cloned.1.call-done = bf16[1024,1024]{1,0:T(8,128)(2,1)} async-done(((bf16[64,1024]{1,0:T(8,128)(2,1)}), bf16[1024,1024]{1,0:T(8,128)(2,1)}) %all-gather.3.cloned.1.call-update) | async-done | bytes 2097168 | tf_op jit(solution)/shard_map/all_gather | solution.py:122
  85.8 4.1 %convolution_convert_fusion.4 = bf16[1024,512]{1,0:T(8,128)(2,1)} fusion(bf16[1024,1024]{1,0:T(8,128)(2,1)} %all-gather.3.cloned.1.call-done, bf16[1024,512]{1,0:T(8,128)(2,1)} %param.28), kind=kOutput, calls=%fused_computation.8 | convolution fusion | flops 1074266112 | bytes 4194304 | tf_op jit(solution)/shard_map/dot_general | solution.py:121
  90.0 76.5 %all-reduce.2.cloned.1.call-done = bf16[1024,512]{1,0:T(8,128)(2,1)} async-done(((bf16[1024,512]{1,0:T(8,128)(2,1)}), bf16[1024,512]{1,0:T(8,128)(2,1)}) %all-reduce.2.cloned.1.call-update) | async-done | bytes 1048592 | tf_op jit(solution)/shard_map/psum | solution.py:129
  166.5 3.2 convert_add_fusion
  169.7 23.6 %psum.15 = f32[1024]{0:T(1024)S(1)} all-reduce(f32[1024]{0:T(1024)S(1)} %get-tuple-element.8), channel_id=1, replica_groups=mesh['attn'=16,'ffn'=8,'grp'=2] {'attn'}, use_global_device_ids=true, to_apply=%region_8.9 | all-reduce | flops 1024 | bytes 8192 | tf_op jit(solution)/shard_map/psum | solution.py:131
  193.4 6.4 %convolution_convert_fusion = bf16[1024,1792]{1,0:T(8,128)(2,1)} fusion(bf16[512,1792]{1,0:T(8,128)(2,1)} %param.30, f32[512]{0:T(512)S(1)} %copy-done.8, f32[1024]{0:T(1024)S(1)} %add_rsqrt_fusion, bf16[1024,512]{1,0:T(8,128)(2,1)} %all-reduce.2.cloned.1.call-done, bf16[1024,512]{1,0:T(8,128)(2,1)} %param.26), kind=kOutput, calls=%fused_computation.1 | convolution fusion | flops 1884028928 | bytes 7608320 | tf_op jit(solution)/shard_map/dot_general | solution.py:141
  199.8 4.2 %convolution_convert_fusion.1 = bf16[1024,1792]{1,0:T(8,128)(2,1)} fusion(bf16[512,1792]{1,0:T(8,128)(2,1)S(1)} %copy-done.7, f32[512]{0:T(512)S(1)} %copy-done.8, f32[1024]{0:T(1024)S(1)} %add_rsqrt_fusion, bf16[1024,512]{1,0:T(8,128)(2,1)S(1)} %copy-done.3, bf16[1024,512]{1,0:T(8,128)(2,1)S(1)} %copy-done.2), kind=kOutput, calls=%fused_computation.2 | convolution fusion | flops 1884028928 | bytes 7608320 | tf_op jit(solution)/shard_map/dot_general | solution.py:140
  204.0 6.6 %pad_maximum_fusion = bf16[1024,3584]{1,0:T(8,128)(2,1)} fusion(bf16[1024,1792]{1,0:T(8,128)(2,1)} %convolution_convert_fusion, bf16[1024,1792]{1,0:T(8,128)(2,1)} %convolution_convert_fusion.1), kind=kLoop, calls=%fused_computation | loop fusion | flops 14680064 | bytes 14680064 | tf_op jit(solution)/shard_map/concatenate | solution.py:138
  210.7 70.3 %reduce-scatter.3.cloned.1.call-done = bf16[64,3584]{1,0:T(8,128)(2,1)} async-done(((bf16[1024,3584]{1,0:T(8,128)(2,1)}), bf16[64,3584]{1,0:T(8,128)(2,1)}) %reduce-scatter.3.cloned.1.call-update) | async-done | bytes 458768 | tf_op jit(solution)/shard_map/reduce_scatter | solution.py:137
  281.0 1.1 convert_element_type.77
  282.1 0.8 fusion.12
  283.0 42.0 %all-gather.5.cloned.1.call-done = bf16[1024,1792]{1,0:T(8,128)(2,1)} async-done(((bf16[64,1792]{1,0:T(8,128)(2,1)}), bf16[1024,1792]{1,0:T(8,128)(2,1)}) %all-gather.5.cloned.1.call-update) | async-done | bytes 3670032 | tf_op jit(solution)/shard_map/all_gather | solution.py:153
  325.0 5.6 %convolution_convert_fusion.5 = bf16[1024,512]{1,0:T(8,128)(2,1)} fusion(bf16[1024,1792]{1,0:T(8,128)(2,1)} %all-gather.5.cloned.1.call-done, bf16[1792,512]{1,0:T(8,128)(2,1)} %param.31), kind=kOutput, calls=%fused_computation.9 | convolution fusion | flops 1879572480 | bytes 6553600 | tf_op jit(solution)/shard_map/dot_general | solution.py:152
  330.6 39.2 %reduce-scatter.5.cloned.1.call-done = bf16[128,512]{1,0:T(8,128)(2,1)} async-done(((bf16[1024,512]{1,0:T(8,128)(2,1)}), bf16[128,512]{1,0:T(8,128)(2,1)}) %reduce-scatter.5.cloned.1.call-update) | async-done | bytes 131088 | tf_op jit(solution)/shard_map/reduce_scatter | solution.py:157
  369.8 1.7 add_convert_fusion
  (40 shorter events, 0.7 us)
Async XLA Ops:
  6.5 18.3 %copy-start = (bf16[64,192,128]{2,1,0:T(8,128)(2,1)S(1)}, bf16[64,192,128]{2,1,0:T(8,128)(2,1)}, u32[]{:S(2)}) copy-start(bf16[64,192,128]{2,1,0:T(8,128)(2,1)} %param.17) | copy-start | bytes 9437188
  10.9 18.6 %all-to-all-start = ((bf16[32,16,128]{2,1,0:T(8,128)(2,1)}), bf16[32,16,128]{2,1,0:T(8,128)(2,1)S(1)}, u32[]{:S(2)}, u32[]{:S(2)}) async-start(bf16[32,16,128]{2,1,0:T(8,128)(2,1)} %bitcast.24), calls=%async_computation | async-start | bytes 262144 | tf_op jit(solution)/shard_map/all_to_all | solution.py:67
  24.8 10.5 %copy-start.4 = (bf16[64,1024]{1,0:T(8,128)(2,1)S(1)}, bf16[64,1024]{1,0:T(8,128)(2,1)}, u32[]{:S(2)}) copy-start(bf16[64,1024]{1,0:T(8,128)(2,1)} %param.16) | copy-start | bytes 393220
  28.0 12.3 %copy-start.5 = (f32[64,1,8]{0,2,1:T(8,128)S(1)}, f32[64,1,8]{0,2,1:T(8,128)}, u32[]{:S(2)}) copy-start(f32[64,1,8]{0,2,1:T(8,128)} %copy.52) | copy-start | bytes 6148
  29.5 15.1 %all-to-all-start.1 = ((bf16[32,16,128]{2,1,0:T(8,128)(2,1)}), bf16[32,16,128]{2,1,0:T(8,128)(2,1)}, u32[]{:S(2)}, u32[]{:S(2)}) async-start(bf16[32,16,128]{2,1,0:T(8,128)(2,1)} %bitcast.28), calls=%async_computation.1 | async-start | bytes 262144 | tf_op jit(solution)/shard_map/all_to_all | solution.py:68
  35.3 50.5 %all-gather.3.cloned.1.call-start = ((), (), s32[]{:S(2)}) async-start(), calls=%async_computation.4 | async-start | bytes 2228224 | tf_op jit(solution)/shard_map/all_gather | solution.py:122
  40.4 3.1 copy-start.1
  40.4 4.3 %copy-start.6 = (f32[64,128]{1,0:T(8,128)S(1)}, f32[64,128]{1,0:T(8,128)}, u32[]{:S(2)}) copy-start(f32[64,128]{1,0:T(8,128)} %convert_element_type.71) | copy-start | bytes 98308
  46.9 119.6 %all-reduce.2.cloned.1.call-start = ((), (), s32[]{:S(2)}) async-start(), calls=%async_computation.5 | async-start | bytes 2097152 | tf_op jit(solution)/shard_map/psum | solution.py:129
  89.9 103.4 %copy-start.8 = (f32[512]{0:T(512)S(1)}, f32[512]{0:T(512)}, u32[]{:S(2)}) copy-start(f32[512]{0:T(512)} %param.27) | copy-start | bytes 6148
  89.9 191.1 %reduce-scatter.3.cloned.1.call-start = ((), (), s32[]{:S(2)}) async-start(), calls=%async_computation.6 | async-start | bytes 7798784 | tf_op jit(solution)/shard_map/reduce_scatter | solution.py:137
  193.3 6.4 %copy-start.2 = (bf16[1024,512]{1,0:T(8,128)(2,1)S(1)}, bf16[1024,512]{1,0:T(8,128)(2,1)}, u32[]{:S(2)}) copy-start(bf16[1024,512]{1,0:T(8,128)(2,1)} %param.26) | copy-start | bytes 3145732
  193.4 6.4 %copy-start.3 = (bf16[1024,512]{1,0:T(8,128)(2,1)S(1)}, bf16[1024,512]{1,0:T(8,128)(2,1)}, u32[]{:S(2)}) copy-start(bf16[1024,512]{1,0:T(8,128)(2,1)} %all-reduce.2.cloned.1.call-done) | copy-start | bytes 3145732
  193.4 6.4 %copy-start.7 = (bf16[512,1792]{1,0:T(8,128)(2,1)S(1)}, bf16[512,1792]{1,0:T(8,128)(2,1)}, u32[]{:S(2)}) copy-start(bf16[512,1792]{1,0:T(8,128)(2,1)} %param.29) | copy-start | bytes 5505028
  210.6 114.3 %all-gather.5.cloned.1.call-start = ((), (), s32[]{:S(2)}) async-start(), calls=%async_computation.7 | async-start | bytes 3899392 | tf_op jit(solution)/shard_map/all_gather | solution.py:153
  282.9 86.8 %reduce-scatter.5.cloned.1.call-start = ((), (), s32[]{:S(2)}) async-start(), calls=%async_computation.8 | async-start | bytes 1179648 | tf_op jit(solution)/shard_map/reduce_scatter | solution.py:157
Sparse Core Ops, SparseCore 0:
  47.0 38.7 all-gather.2
  90.0 76.4 all-reduce.1
  210.8 70.1 reduce-scatter.2
  283.0 41.8 all-gather.4
  330.7 38.9 reduce-scatter.4
where the time goes:
time: 379 us; the launch traced here: 378 us
  waiting for transfers between devices  267 us (70%)
  matrix products  32.3 us (9%)
  other arithmetic  23.7 us (6%)
  blocking collectives  23.6 us (6%)
  between operations  13.3 us (4%)
  starting transfers between devices  11.8 us (3%)
  local copies, waits for them, and re-layouts  6.4 us (2%)
    psum x1, waiting for transfers between devices, body(): lax.psum(head_part.astype(jnp.bfloat16), 'ffn').astype(jnp.float32)  76.5 us
    reduce_scatter x1, waiting for transfers between devices, body(): lax.psum_scatter(jnp.concatenate([jnp.dot(normed, w_gate, preferred_eleme...  70.3 us
    all_gather x1, waiting for transfers between devices, body(): lax.all_gather(activated, 'attn', axis=0, tiled=True)  42 us
    reduce_scatter x1, waiting for transfers between devices, body(): lax.psum_scatter(down_part.astype(jnp.bfloat16), 'ffn', scatter_dimension...  39.2 us
    all_gather x1, waiting for transfers between devices, body(): lax.all_gather(attended, 'attn', axis=0, tiled=True)  38.8 us
    psum x1, blocking collectives, body(): squares = lax.psum(jnp.sum(mixed * mixed, axis=1), 'attn')  23.6 us
  transfers between devices with their start and end apart: 7, of which 5 were waited for; matrix products, arithmetic and copies ran while one was open for 6% of the time, Pallas kernels for 0%

commit v1 on v0

--- a/solution.py
+++ b/solution.py
@@ -1,3 +1,4 @@
+import functools
 import jax
 import jax.numpy as jnp
 from jax import lax
@@ -9,6 +10,14 @@
 HEAD_SIZE = 128
 CAP = 2
 epsilon = 1e-05
+
+
+def track_the_field(state, a_name):
+    all_values = jnp.sum(jax.lax.all_gather(state, a_name), axis=0)
+    return all_values
+
+
+_store_forms = functools.partial(track_the_field, a_name="ffn")
 
 
 def body(
@@ -126,7 +135,7 @@
     ffn_size = lax.axis_size("ffn")
     ffn_index = lax.axis_index("ffn")
     share_rows = head_part.shape[0] // ffn_size
-    attn_out = lax.psum(head_part.astype(jnp.bfloat16), "ffn").astype(jnp.float32)
+    attn_out = _store_forms(head_part.astype(jnp.bfloat16)).astype(jnp.float32)
     mixed = residual.astype(jnp.float32) + attn_out
     squares = lax.psum(jnp.sum(mixed * mixed, axis=1), "attn")
     normed = (mixed * lax.rsqrt(squares / MODEL_WIDTH + epsilon)[:, None] * norm_gain).astype(

time: 379 us -> 406 us (1.071)
  waiting for transfers between devices: 267 us -> 286 us
  other arithmetic: 23.7 us -> 29.5 us
    all_gather x0 -> x1, waiting for transfers between devices: none -> 94.8 us  [track_the_field(): all_values = jnp.sum(jax.lax.all_gather(state, a_name), axis=0)]
    psum x1 -> x0, waiting for transfers between devices: 76.5 us -> none  [body(): lax.psum(head_part.astype(jnp.bfloat16), 'ffn').astype(jnp.float32)]
    reduce_sum x0 -> x1, other arithmetic: none -> 5.86 us  [track_the_field(): all_values = jnp.sum(jax.lax.all_gather(state, a_name), axis=0)]
  transfers between devices with their start and end apart: 7 -> 7, of which waited for: 5 -> 5; matrix products, arithmetic and copies ran while one was open for 6% -> 5% of each run, Pallas kernels for 0% -> 0%
where the time goes in v1:
time: 406 us
  waiting for transfers between devices  286 us (70%)
  matrix products  32.4 us (8%)
  other arithmetic  29.5 us (7%)
  blocking collectives  26.5 us (7%)
  between operations  13.3 us (3%)
  starting transfers between devices  11.8 us (3%)
  local copies, waits for them, and re-layouts  6.39 us (2%)
    all_gather x1, waiting for transfers between devices, track_the_field(): all_values = jnp.sum(jax.lax.all_gather(state, a_name), axis=0)  94.8 us
    reduce_scatter x1, waiting for transfers between devices, body(): lax.psum_scatter(jnp.concatenate([jnp.dot(normed, w_gate, preferred_eleme...  70.6 us
    all_gather x1, waiting for transfers between devices, body(): lax.all_gather(activated, 'attn', axis=0, tiled=True)  42.1 us
    reduce_scatter x1, waiting for transfers between devices, body(): lax.psum_scatter(down_part.astype(jnp.bfloat16), 'ffn', scatter_dimension...  39.2 us
    all_gather x1, waiting for transfers between devices, body(): lax.all_gather(attended, 'attn', axis=0, tiled=True)  38.8 us
    psum x1, blocking collectives, body(): squares = lax.psum(jnp.sum(mixed * mixed, axis=1), 'attn')  26.5 us
  transfers between devices with their start and end apart: 7, of which 5 were waited for; matrix products, arithmetic and copies ran while one was open for 5% of the time, Pallas kernels for 0%

profile of v1, /device:TPU:2, one launch (start us, length us, event | category | flops | bytes accessed | tf_op | source)
XLA Modules:
  0.0 405.6 jit_solution(8091418922527118570)
XLA Ops:
  6.5 0.5 broadcast.96
  7.1 1.6 reduce.10
  8.7 0.4 convert_reduce_fusion
  9.2 1.0 fusion.6
  10.2 0.7 copy.58
  10.9 5.9 %all-to-all-start = ((bf16[32,16,128]{2,1,0:T(8,128)(2,1)}), bf16[32,16,128]{2,1,0:T(8,128)(2,1)S(1)}, u32[]{:S(2)}, u32[]{:S(2)}) async-start(bf16[32,16,128]{2,1,0:T(8,128)(2,1)} %bitcast.25), calls=%async_computation | async-start | bytes 262144 | tf_op jit(solution)/shard_map/all_to_all | solution.py:76
  16.8 0.7 broadcast_add_fusion.1
  17.5 0.1 select_reduce_fusion
  17.7 0.1 sub.28
  17.9 0.7 eq.78
  18.6 0.7 iota_compare_fusion.1
  19.3 1.3 convert_element_type.73
  20.6 1.0 fusion.7
  21.6 0.7 copy.60
  22.3 0.9 copy.56
  23.2 0.9 fusion.21
  24.2 0.7 copy.52
  24.8 3.2 fusion.30
  28.0 0.8 copy.45
  28.8 0.7 iota_compare_fusion
  29.5 5.7 %all-to-all-start.1 = ((bf16[32,16,128]{2,1,0:T(8,128)(2,1)}), bf16[32,16,128]{2,1,0:T(8,128)(2,1)}, u32[]{:S(2)}, u32[]{:S(2)}) async-start(bf16[32,16,128]{2,1,0:T(8,128)(2,1)} %bitcast.29), calls=%async_computation.1 | async-start | bytes 262144 | tf_op jit(solution)/shard_map/all_to_all | solution.py:77
  35.3 1.3 fusion.31
  36.6 0.7 maximum_maximum_fusion
  37.3 0.1 copy.46
  37.4 1.5 fusion.8
  38.9 1.3 fusion.11
  40.3 0.1 copy.48
  40.4 3.1 convolution_bitcast_fusion.1
  43.5 1.1 fusion.10
  44.6 0.1 copy.50
  44.7 1.5 fusion.5
  46.2 0.7 copy.81
  47.0 38.8 %all-gather.5.cloned.1.call-done = bf16[1024,1024]{1,0:T(8,128)(2,1)} async-done(((bf16[64,1024]{1,0:T(8,128)(2,1)}), bf16[1024,1024]{1,0:T(8,128)(2,1)}) %all-gather.5.cloned.1.call-update) | async-done | bytes 2097168 | tf_op jit(solution)/shard_map/all_gather | solution.py:131
  85.8 4.2 %convolution_convert_fusion.4 = bf16[1024,512]{1,0:T(8,128)(2,1)} fusion(bf16[1024,1024]{1,0:T(8,128)(2,1)} %all-gather.5.cloned.1.call-done, bf16[1024,512]{1,0:T(8,128)(2,1)} %param.28), kind=kOutput, calls=%fused_computation.8 | convolution fusion | flops 1074266112 | bytes 4194304 | tf_op jit(solution)/shard_map/dot_general | solution.py:130
  90.0 94.8 %all-gather.9.cloned.1.call-done = bf16[8192,512]{1,0:T(8,128)(2,1)} async-done(((bf16[1024,512]{1,0:T(8,128)(2,1)}), bf16[8192,512]{1,0:T(8,128)(2,1)}) %all-gather.9.cloned.1.call-update) | async-done | bytes 8388624 | tf_op jit(solution)/shard_map/all_gather | solution.py:16
  184.8 5.9 %reduce_sum.61 = bf16[1024,512]{1,0:T(8,128)(2,1)} reduce(bf16[8,1024,512]{2,1,0:T(8,128)(2,1)} %bitcast.85, bf16[]{:T(256)} %constant.41.clone.1), dimensions={0}, to_apply=%region_6.7 | reduce | flops 3670016 | bytes 9437186 | tf_op jit(solution)/shard_map/reduce_sum | solution.py:16
  190.7 3.2 convert_add_fusion
  193.9 26.5 %psum.7 = f32[1024]{0:T(1024)S(1)} all-reduce(f32[1024]{0:T(1024)S(1)} %get-tuple-element.8), channel_id=1, replica_groups=mesh['attn'=16,'ffn'=8,'grp'=2] {'attn'}, use_global_device_ids=true, to_apply=%region_8.9 | all-reduce | flops 1024 | bytes 8192 | tf_op jit(solution)/shard_map/psum | solution.py:140
  220.5 6.4 %convolution_convert_fusion = bf16[1024,1792]{1,0:T(8,128)(2,1)} fusion(bf16[512,1792]{1,0:T(8,128)(2,1)} %param.30, f32[512]{0:T(512)S(1)} %copy-done.8, f32[1024]{0:T(1024)S(1)} %add_rsqrt_fusion, bf16[1024,512]{1,0:T(8,128)(2,1)} %reduce_sum.61, bf16[1024,512]{1,0:T(8,128)(2,1)} %param.26), kind=kOutput, calls=%fused_computation.1 | convolution fusion | flops 1884028928 | bytes 7608320 | tf_op jit(solution)/shard_map/dot_general | solution.py:150
  226.9 4.2 %convolution_convert_fusion.1 = bf16[1024,1792]{1,0:T(8,128)(2,1)} fusion(bf16[512,1792]{1,0:T(8,128)(2,1)S(1)} %copy-done.7, f32[512]{0:T(512)S(1)} %copy-done.8, f32[1024]{0:T(1024)S(1)} %add_rsqrt_fusion, bf16[1024,512]{1,0:T(8,128)(2,1)S(1)} %copy-done.2, bf16[1024,512]{1,0:T(8,128)(2,1)S(1)} %copy-done.3), kind=kOutput, calls=%fused_computation.2 | convolution fusion | flops 1884028928 | bytes 7608320 | tf_op jit(solution)/shard_map/dot_general | solution.py:149
  231.1 6.6 %pad_maximum_fusion = bf16[1024,3584]{1,0:T(8,128)(2,1)} fusion(bf16[1024,1792]{1,0:T(8,128)(2,1)} %convolution_convert_fusion, bf16[1024,1792]{1,0:T(8,128)(2,1)} %convolution_convert_fusion.1), kind=kLoop, calls=%fused_computation | loop fusion | flops 14680064 | bytes 14680064 | tf_op jit(solution)/shard_map/concatenate | solution.py:147
  237.8 70.6 %reduce-scatter.3.cloned.1.call-done = bf16[64,3584]{1,0:T(8,128)(2,1)} async-done(((bf16[1024,3584]{1,0:T(8,128)(2,1)}), bf16[64,3584]{1,0:T(8,128)(2,1)}) %reduce-scatter.3.cloned.1.call-update) | async-done | bytes 458768 | tf_op jit(solution)/shard_map/reduce_scatter | solution.py:146
  308.4 1.1 convert_element_type.79
  309.5 0.8 fusion.12
  310.4 42.1 %all-gather.7.cloned.1.call-done = bf16[1024,1792]{1,0:T(8,128)(2,1)} async-done(((bf16[64,1792]{1,0:T(8,128)(2,1)}), bf16[1024,1792]{1,0:T(8,128)(2,1)}) %all-gather.7.cloned.1.call-update) | async-done | bytes 3670032 | tf_op jit(solution)/shard_map/all_gather | solution.py:162
  352.5 5.6 %convolution_convert_fusion.5 = bf16[1024,512]{1,0:T(8,128)(2,1)} fusion(bf16[1024,1792]{1,0:T(8,128)(2,1)} %all-gather.7.cloned.1.call-done, bf16[1792,512]{1,0:T(8,128)(2,1)} %param.31), kind=kOutput, calls=%fused_computation.9 | convolution fusion | flops 1879572480 | bytes 6553600 | tf_op jit(solution)/shard_map/dot_general | solution.py:161
  358.2 39.2 %reduce-scatter.5.cloned.1.call-done = bf16[128,512]{1,0:T(8,128)(2,1)} async-done(((bf16[1024,512]{1,0:T(8,128)(2,1)}), bf16[128,512]{1,0:T(8,128)(2,1)}) %reduce-scatter.5.cloned.1.call-update) | async-done | bytes 131088 | tf_op jit(solution)/shard_map/reduce_scatter | solution.py:166
  397.4 1.7 add_convert_fusion
  (41 shorter events, 0.8 us)
Async XLA Ops:
  6.5 18.3 %copy-start = (bf16[64,192,128]{2,1,0:T(8,128)(2,1)S(1)}, bf16[64,192,128]{2,1,0:T(8,128)(2,1)}, u32[]{:S(2)}) copy-start(bf16[64,192,128]{2,1,0:T(8,128)(2,1)} %param.17) | copy-start | bytes 9437188
  10.9 18.6 %all-to-all-start = ((bf16[32,16,128]{2,1,0:T(8,128)(2,1)}), bf16[32,16,128]{2,1,0:T(8,128)(2,1)S(1)}, u32[]{:S(2)}, u32[]{:S(2)}) async-start(bf16[32,16,128]{2,1,0:T(8,128)(2,1)} %bitcast.25), calls=%async_computation | async-start | bytes 262144 | tf_op jit(solution)/shard_map/all_to_all | solution.py:76
  24.8 10.5 %copy-start.4 = (bf16[64,1024]{1,0:T(8,128)(2,1)S(1)}, bf16[64,1024]{1,0:T(8,128)(2,1)}, u32[]{:S(2)}) copy-start(bf16[64,1024]{1,0:T(8,128)(2,1)} %param.16) | copy-start | bytes 393220
  28.0 12.3 %copy-start.5 = (f32[64,1,8]{0,2,1:T(8,128)S(1)}, f32[64,1,8]{0,2,1:T(8,128)}, u32[]{:S(2)}) copy-start(f32[64,1,8]{0,2,1:T(8,128)} %copy.52) | copy-start | bytes 6148
  29.5 15.1 %all-to-all-start.1 = ((bf16[32,16,128]{2,1,0:T(8,128)(2,1)}), bf16[32,16,128]{2,1,0:T(8,128)(2,1)}, u32[]{:S(2)}, u32[]{:S(2)}) async-start(bf16[32,16,128]{2,1,0:T(8,128)(2,1)} %bitcast.29), calls=%async_computation.1 | async-start | bytes 262144 | tf_op jit(solution)/shard_map/all_to_all | solution.py:77
  35.3 50.5 %all-gather.5.cloned.1.call-start = ((), (), s32[]{:S(2)}) async-start(), calls=%async_computation.4 | async-start | bytes 2228224 | tf_op jit(solution)/shard_map/all_gather | solution.py:131
  40.4 3.1 copy-start.1
  40.4 4.3 %copy-start.6 = (f32[64,128]{1,0:T(8,128)S(1)}, f32[64,128]{1,0:T(8,128)}, u32[]{:S(2)}) copy-start(f32[64,128]{1,0:T(8,128)} %convert_element_type.73) | copy-start | bytes 98308
  46.9 137.9 %all-gather.9.cloned.1.call-start = ((), (), s32[]{:S(2)}) async-start(), calls=%async_computation.8 | async-start | bytes 9437184 | tf_op jit(solution)/shard_map/all_gather | solution.py:16
  90.0 218.4 %reduce-scatter.3.cloned.1.call-start = ((), (), s32[]{:S(2)}) async-start(), calls=%async_computation.5 | async-start | bytes 7798784 | tf_op jit(solution)/shard_map/reduce_scatter | solution.py:146
  190.7 29.7 %copy-start.8 = (f32[512]{0:T(512)S(1)}, f32[512]{0:T(512)}, u32[]{:S(2)}) copy-start(f32[512]{0:T(512)} %param.27) | copy-start | bytes 6148
  220.4 6.4 %copy-start.2 = (bf16[1024,512]{1,0:T(8,128)(2,1)S(1)}, bf16[1024,512]{1,0:T(8,128)(2,1)}, u32[]{:S(2)}) copy-start(bf16[1024,512]{1,0:T(8,128)(2,1)} %reduce_sum.61) | copy-start | bytes 3145732
  220.4 6.4 %copy-start.3 = (bf16[1024,512]{1,0:T(8,128)(2,1)S(1)}, bf16[1024,512]{1,0:T(8,128)(2,1)}, u32[]{:S(2)}) copy-start(bf16[1024,512]{1,0:T(8,128)(2,1)} %param.26) | copy-start | bytes 3145732
  220.5 6.4 %copy-start.7 = (bf16[512,1792]{1,0:T(8,128)(2,1)S(1)}, bf16[512,1792]{1,0:T(8,128)(2,1)}, u32[]{:S(2)}) copy-start(bf16[512,1792]{1,0:T(8,128)(2,1)} %param.29) | copy-start | bytes 5505028
  237.7 114.8 %all-gather.7.cloned.1.call-start = ((), (), s32[]{:S(2)}) async-start(), calls=%async_computation.6 | async-start | bytes 3899392 | tf_op jit(solution)/shard_map/all_gather | solution.py:162
  310.3 87.0 %reduce-scatter.5.cloned.1.call-start = ((), (), s32[]{:S(2)}) async-start(), calls=%async_computation.7 | async-start | bytes 1179648 | tf_op jit(solution)/shard_map/reduce_scatter | solution.py:166
Sparse Core Ops, SparseCore 0:
  47.0 38.7 all-gather.4
  90.1 94.6 all-gather.8
  237.8 70.5 reduce-scatter.2
  310.5 42.0 all-gather.6
  358.3 39.0 reduce-scatter.4
